TPU v7x, 32 devices: a whole 2x2x4 slice. The times are simulated.
32 devices in a mesh: space: 4 (over x, core), chaos: 8 (over z, y).
Axes of the slice: x: 2, y: 2, z: 4, core: 2. Of those that a mesh axis runs over, the one named last changes fastest.
Arguments:
- chaos_field: bfloat16 [256, 32, 16, 128], P('chaos', 'space'), may hold values from -6 to 6
- conductivity: float32 [11, 32, 16, 128], P(None, 'space', 'chaos'), may hold values from 0.1 to 1
- triple_tensor: bfloat16 [11, 256, 256], replicated, may hold values from -0.02734375 to 0.02734375
- block_pattern: int32 [8, 8], replicated, may hold values 0 or 1
Outputs:
- first: bfloat16 [256, 32, 16, 128], P('chaos', 'space')
- second: bfloat16 [256, 32, 16, 128], P('chaos', 'space')
All inputs are finite; a program needn't handle non-finite values.
Results may differ from a plain program's by a relative error of at most 0.0043.
Values may be sent and summed in bfloat16 or wider, within the bound.
A program may use at most 128 MiB of HBM per device.

v0:
```python
import jax
import jax.numpy as jnp
from jax import lax
from jax.sharding import PartitionSpec as P


def padded_2(shard, sides, width):
    for axis, dim in sides:
        peers, length = (lax.axis_size(axis), shard.shape[dim])
        up = [(i, (i + 1) % peers) for i in range(peers - 1)]
        down = [(j, i) for i, j in up]
        last = lax.slice_in_dim(shard, length - width, length, axis=dim)
        first = lax.slice_in_dim(shard, 0, width, axis=dim)
        before = lax.ppermute(last, axis, up)
        after = lax.ppermute(first, axis, down)
        shard = jnp.concatenate([before, shard, after], axis=dim)
    return shard


def neighbours(padded):
    centre = padded[..., 1:-1, :, :]
    lead = [(0, 0)] * (centre.ndim - 2)
    ypad = jnp.pad(centre, lead + [(1, 1), (0, 0)])
    zpad = jnp.pad(centre, lead + [(0, 0), (1, 1)])
    return (
        centre,
        [
            padded[..., :-2, :, :],
            padded[..., 2:, :, :],
            ypad[..., :-2, :],
            ypad[..., 2:, :],
            zpad[..., :-2],
            zpad[..., 2:],
        ],
    )


def local(chaos_field, conductivity, triple_tensor, block_pattern):
    local_rows = chaos_field.shape[0]
    block_size = triple_tensor.shape[1] // block_pattern.shape[0]
    own_index = lax.axis_index("chaos")
    expanded = jnp.repeat(jnp.repeat(block_pattern, block_size, 0), block_size, 1).astype(
        triple_tensor.dtype
    )
    masked = triple_tensor * expanded[None]
    gathered = lax.all_gather(conductivity, "chaos", axis=2, tiled=True)
    kpad = padded_2(gathered, (("space", 1),), 1)
    kcentre, knear = neighbours(kpad)
    faces = [0.5 * (kcentre + other) for other in knear]
    face_total = faces[0] + faces[1] + faces[2] + faces[3] + faces[4] + faces[5]

    def product(field):
        padded = padded_2(field, (("space", 1),), 1).astype(jnp.float32)
        centre, near = neighbours(padded)
        applied = face_total[:, None] * centre[None]
        for index in range(6):
            applied = applied - faces[index][:, None] * near[index][None]
        columns = lax.dynamic_slice_in_dim(masked, own_index * local_rows, local_rows, 2).astype(
            jnp.float32
        )
        return lax.psum_scatter(
            jnp.einsum("kij,kjxyz->ixyz", columns, applied, precision=lax.Precision.HIGHEST),
            "chaos",
            scatter_dimension=0,
            tiled=True,
        )

    first = product(chaos_field).astype(jnp.bfloat16)
    second = product(first).astype(jnp.bfloat16)
    return (first, second)


def solution(mesh):
    return jax.shard_map(
        local,
        mesh=mesh,
        in_specs=(P("chaos", "space", None, None), P(None, "space", "chaos", None), P(), P()),
        out_specs=(P("chaos", "space", None, None), P("chaos", "space", None, None)),
        check_vma=False,
    )
```

profile of v0, /device:TPU:0, one launch (start us, length us, event | category | flops | bytes accessed | tf_op | source)
XLA Modules:
  0.0 726.1 jit_solution(2191133068551779548)
XLA Ops:
  7.2 1.8 fusion.89
  9.0 3.0 collective-permute-start.2
  12.0 1.3 collective-permute-start.3
  14.2 33.1 %all_gather.3 = f32[11,8,16,128]{3,1,0,2:T(8,128)S(1)} all-gather(f32[11,8,2,128]{3,1,0,2:T(8,128)S(1)} %copy.26), channel_id=1, replica_groups=mesh['space'=4,'chaos'=8] {'chaos'}, dimensions={2}, use_global_device_ids=true | all-gather | bytes 811008 | tf_op jit(solution)/shard_map/all_gather | solution.py:46
  47.4 1.3 collective-permute-start.1
  48.7 3.0 collective-permute-start
  54.8 1.2 copy.29
  56.0 1.2 copy.31
  58.3 1.2 copy.35
  59.4 1.1 copy.37
  60.6 1.1 copy.39
  61.7 1.2 maximum_convert_fusion
  63.5 1.2 copy.28
  64.7 1.8 pad_slice_fusion.5
  66.6 1.2 copy.30
  67.8 1.2 copy.32
  69.0 1.2 copy.34
  70.2 1.2 copy.36
  71.5 1.4 copy.40
  72.9 1.2 copy.38
  75.1 29.1 %fusion.56 = f32[256,8,16,128]{3,0,2,1:T(8,128)} fusion(f32[32,8,16,128]{3,0,2,1:T(8,128)S(1)} %copy.40, f32[11,8,16,128]{3,0,2,1:T(8,128)S(1)} %copy-done.12, f32[32,8,16,128]{3,0,2,1:T(8,128)S(1)} %copy.38, f32[11,8,16,128]{3,0,2,1:T(8,128)S(1)} %copy-done.10, f32[32,8,16,128]{3,0,2,1:T(8,128)S(1)} %copy.36, f32[11,8,16,128]{3,0,2,1:T(8,128)S(1)} %copy-done.8, ...), kind=kOutput, calls=%fused_computation.56 | convolution fusion | flops 17792073728 | bytes 36700160 | tf_op jit(solution)/shard_map/kij,kjxyz->ixyz/dot_general | solution.py:62
  104.2 287.0 %reduce-scatter.3.cloned.1.call-done = f32[32,8,16,128]{3,0,2,1:T(8,128)} async-done(((f32[256,8,16,128]{3,0,2,1:T(8,128)}), f32[32,8,16,128]{3,0,2,1:T(8,128)}) %reduce-scatter.3.cloned.1.call-update) | async-done | bytes 2097168 | tf_op jit(solution)/shard_map/reduce_scatter | solution.py:61
  391.2 1.8 convert_element_type.43
  393.0 1.8 collective-permute-start.4
  394.9 1.3 collective-permute-start.5
  396.2 3.1 collective-permute-done.5
  400.4 1.6 pad_slice_fusion.7
  402.8 29.0 %fusion.59 = f32[256,8,16,128]{3,0,2,1:T(8,128)} fusion(f32[32,8,16,128]{3,0,2,1:T(8,128)S(1)} %get-tuple-element.21, f32[32,8,16,128]{3,0,2,1:T(8,128)S(1)} %get-tuple-element.22, f32[32,8,16,128]{3,0,2,1:T(8,128)S(1)} %get-tuple-element.20, f32[32,8,16,128]{3,0,2,1:T(8,128)S(1)} %get-tuple-element.19, f32[32,8,16,128]{3,0,2,1:T(8,128)S(1)} %get-tuple-element.14, ...), kind=kOutput, calls=%fused_computation.57 | convolution fusion | flops 17792073728 | bytes 36700160 | tf_op jit(solution)/shard_map/kij,kjxyz->ixyz/dot_general | solution.py:62
  431.9 1.4 copy.41
  433.2 282.8 %reduce-scatter.5.cloned.1.call-done = f32[32,8,16,128]{3,0,2,1:T(8,128)} async-done(((f32[256,8,16,128]{3,0,2,1:T(8,128)}), f32[32,8,16,128]{3,0,2,1:T(8,128)}) %reduce-scatter.5.cloned.1.call-update) | async-done | bytes 2097168 | tf_op jit(solution)/shard_map/reduce_scatter | solution.py:61
  716.0 1.8 convert_element_type.45
  717.8 1.4 copy.42
  (56 shorter events, 8.7 us)
Async XLA Ops:
  7.2 45.5 %copy-start = (bf16[11,256,256]{2,1,0:T(8,128)(2,1)S(1)}, bf16[11,256,256]{2,1,0:T(8,128)(2,1)}, u32[]{:S(2)}) copy-start(bf16[11,256,256]{2,1,0:T(8,128)(2,1)} %param.6) | copy-start | bytes 4325380
  7.2 384.0 %reduce-scatter.3.cloned.1.call-start = ((), (), s32[]{:S(2)}) async-start(), calls=%async_computation.2 | async-start | bytes 18874368 | tf_op jit(solution)/shard_map/reduce_scatter | solution.py:61
  9.0 52.7 %collective-permute-start.2 = (bf16[32,1,16,128]{3,2,1,0:T(8,128)(2,1)}, bf16[32,1,16,128]{3,2,1,0:T(8,128)(2,1)}, u32[]{:S(2)}, u32[]{:S(2)}) collective-permute-start(bf16[32,1,16,128]{3,2,1,0:T(8,128)(2,1)} %get-tuple-element.29), channel_id=1, source_target_pairs={{0,8},{8,16},{16,24},{1,9},{9,17},{17,25},{2,10},{10,18},{18,26},{... | collective-permute-start | bytes 393224 | tf_op jit(solution)/shard_map/ppermute | solution.py:14
  12.0 49.7 %collective-permute-start.3 = (bf16[32,1,16,128]{3,2,1,0:T(8,128)(2,1)}, bf16[32,1,16,128]{3,2,1,0:T(8,128)(2,1)}, u32[]{:S(2)}, u32[]{:S(2)}) collective-permute-start(bf16[32,1,16,128]{3,2,1,0:T(8,128)(2,1)} %get-tuple-element.30), channel_id=1, source_target_pairs={{8,0},{16,8},{24,16},{9,1},{17,9},{25,17},{10,2},{18,10},{26,18},{... | collective-permute-start | bytes 393224 | tf_op jit(solution)/shard_map/ppermute | solution.py:15
  47.4 6.5 collective-permute-start.1
  48.7 5.2 collective-permute-start
  59.4 2.3 copy-start.2
  71.5 2.7 copy-start.10
  71.5 2.7 copy-start.12
  71.5 2.7 copy-start.14
  72.9 1.3 copy-start.3
  72.9 1.6 copy-start.4
  72.9 1.9 copy-start.6
  72.9 2.2 copy-start.8
  104.2 611.8 %reduce-scatter.5.cloned.1.call-start = ((), (), s32[]{:S(2)}) async-start(), calls=%async_computation.3 | async-start | bytes 18874368 | tf_op jit(solution)/shard_map/reduce_scatter | solution.py:61
  393.0 3.1 collective-permute-start.4
  394.9 4.4 collective-permute-start.5
  400.3 1.7 copy-start.5
  400.3 1.7 copy-start.7
  400.3 1.8 copy-start.9
  400.4 2.2 copy-start.11
  400.4 2.5 copy-start.13
  431.8 287.4 %copy-start.1 = (bf16[11,256,256]{2,1,0:T(8,128)(2,1)S(1)}, bf16[11,256,256]{2,1,0:T(8,128)(2,1)}, u32[]{:S(2)}) copy-start(bf16[11,256,256]{2,1,0:T(8,128)(2,1)} %param.6) | copy-start | bytes 4325380
Sparse Core Ops, SparseCore 0:
  104.3 286.8 reduce-scatter.2
  432.0 284.0 reduce-scatter.4
where the time goes:
time: 726 us
  waiting for transfers between devices  573 us (79%)
  matrix products  58.1 us (8%)
  blocking collectives  33.1 us (5%)
  local copies, waits for them, and re-layouts  29.4 us (4%)
  between operations  14.4 us (2%)
  starting transfers between devices  11.8 us (2%)
    reduce_scatter x2, waiting for transfers between devices, product(): lax.psum_scatter(jnp.einsum('kij,kjxyz->ixyz', columns, applied, precisio...  570 us
    dot_general x2, matrix products, product(): jnp.einsum('kij,kjxyz->ixyz', columns, applied, precision=lax.Precision.H...  58.1 us
    all_gather x1, blocking collectives, local(): gathered = lax.all_gather(conductivity, 'chaos', axis=2, tiled=True)  33.1 us
  transfers between devices with their start and end apart: 8, of which 3 were waited for; matrix products, arithmetic and copies ran while one was open for 2% of the time, Pallas kernels for 0%

commit v1 on v0

v1 whole, which is shorter than its diff:
```python
import functools

import jax
import jax.numpy as jnp
from jax import lax
from jax.experimental import pallas as pl
from jax.experimental.pallas import tpu as pltpu
from jax.sharding import PartitionSpec as P

MESH = pl.DeviceIdType.MESH
TILE = 64


def kernel(
    n, slabs, modes, vt, tensor, mask, kt, out1, out2,
    vbuf, fbuf, sbuf, kbuf, skap, m2, acc, w, wy,
    in_send, in_recv, khalo_send, khalo_recv, vhalo_send, vhalo_recv, fhalo_send, fhalo_recv,
    out_send, out_recv, local_sem,
):
    me = lax.axis_index("chaos")
    sp = lax.axis_index("space")
    yl, nx = vbuf.shape[0] - 2, vbuf.shape[1] - 2
    coeffs, nz = vbuf.shape[2], vbuf.shape[3]
    cl = coeffs // n
    tiles = coeffs // TILE
    f32, bf16 = jnp.float32, jnp.bfloat16

    down, up = me > 0, me < n - 1
    left, right = sp > 0, sp < slabs - 1

    for buf in (vbuf, fbuf, kbuf):
        @pl.when(jnp.logical_not(down))
        def _(buf=buf):
            buf[0] = jnp.zeros(buf.shape[1:], buf.dtype)

        @pl.when(jnp.logical_not(up))
        def _(buf=buf):
            buf[yl + 1] = jnp.zeros(buf.shape[1:], buf.dtype)

        @pl.when(jnp.logical_not(left))
        def _(buf=buf):
            for y in range(yl):
                buf[1 + y, 0] = jnp.zeros(buf.shape[2:], buf.dtype)

        @pl.when(jnp.logical_not(right))
        def _(buf=buf):
            for y in range(yl):
                buf[1 + y, nx + 1] = jnp.zeros(buf.shape[2:], buf.dtype)

    for y in range(yl):
        for x in range(nx):
            kbuf[1 + y, 1 + x] = kt[y, x]

    barrier = pltpu.get_barrier_semaphore()

    @pl.loop(1, n)
    def _(s):
        pl.semaphore_signal(barrier, inc=1, device_id={"chaos": lax.rem(me + s, n)}, device_id_type=MESH)

    @pl.when(left)
    def _():
        pl.semaphore_signal(barrier, inc=1, device_id={"space": sp - 1}, device_id_type=MESH)

    @pl.when(right)
    def _():
        pl.semaphore_signal(barrier, inc=1, device_id={"space": sp + 1}, device_id_type=MESH)

    pl.semaphore_wait(barrier, n - 1 + left.astype(jnp.int32) + right.astype(jnp.int32))

    def in_copy(d, src_dev, peer):
        return pltpu.make_async_remote_copy(
            src_ref=vt.at[pl.ds(d * yl, yl)],
            dst_ref=vbuf.at[pl.ds(1, yl), pl.ds(1, nx), pl.ds(pl.multiple_of(src_dev * cl, cl), cl)],
            send_sem=in_send.at[d], recv_sem=in_recv.at[src_dev],
            device_id={"chaos": peer}, device_id_type=MESH,
        )

    @pl.loop(1, n)
    def _(s):
        d = lax.rem(me + s, n)
        in_copy(d, me, d).start()

    own_in = pltpu.make_async_copy(
        vt.at[pl.ds(me * yl, yl)],
        vbuf.at[pl.ds(1, yl), pl.ds(1, nx), pl.ds(pl.multiple_of(me * cl, cl), cl)],
        local_sem.at[0],
    )
    own_in.start()

    inner, rows = pl.ds(1, nx), pl.ds(1, yl)
    other = lax.rem(me + 1, n)

    def halo(buf, send, recv, index, target, xs=None):
        at = inner if xs is None else xs
        if index == 0:
            src, dst = buf.at[1, at], buf.at[yl + 1, at]
        elif index == 1:
            src, dst = buf.at[yl, at], buf.at[0, at]
        elif index == 2:
            src, dst = buf.at[rows, 1], buf.at[rows, nx + 1]
        else:
            src, dst = buf.at[rows, nx], buf.at[rows, 0]
        return pltpu.make_async_remote_copy(
            src_ref=src, dst_ref=dst, send_sem=send.at[index], recv_sem=recv.at[index],
            device_id=target, device_id_type=MESH,
        )

    sends = [
        (down, {"chaos": me - 1}), (up, {"chaos": me + 1}),
        (left, {"space": sp - 1}), (right, {"space": sp + 1}),
    ]
    arrives = [up, down, right, left]

    def halo_start(buf, send, recv, index, xs=None):
        cond, target = sends[index]

        @pl.when(cond)
        def _():
            halo(buf, send, recv, index, target, xs).start()

    def halo_wait_recv(buf, send, recv):
        for index in range(4):
            @pl.when(arrives[index])
            def _(index=index):
                halo(buf, send, recv, index, {"chaos": other}).wait_recv()

    def halo_wait_send(buf, send, recv):
        for index in range(4):
            @pl.when(sends[index][0])
            def _(index=index):
                halo(buf, send, recv, index, {"chaos": other}).wait_send()

    for index in range(4):
        halo_start(kbuf, khalo_send, khalo_recv, index)

    @pl.loop(0, tiles)
    def _(it):
        at = pl.ds(pl.multiple_of(it * TILE, TILE), TILE)
        part = mask[at]
        for k in range(modes):
            value = tensor[k, at] * part
            m2[it, k * TILE:(k + 1) * TILE, :coeffs] = value
            m2[it, k * TILE:(k + 1) * TILE, coeffs:] = value

    lane = lax.broadcasted_iota(jnp.int32, (1, nz), 1)

    def zsum(block):
        before = jnp.where(lane == 0, 0.0, pltpu.roll(block, 1, 1))
        after = jnp.where(lane == nz - 1, 0.0, pltpu.roll(block, nz - 1, 1))
        return before + after

    def row(buf, x, first=1):
        return jnp.concatenate([buf[first + y, x] for y in range(yl)], axis=1)

    halo_wait_recv(kbuf, khalo_send, khalo_recv)

    @pl.loop(0, nx)
    def _(x):
        parts = []
        for y in range(yl):
            parts.append(
                kbuf[1 + y, x] + kbuf[1 + y, x + 2] + kbuf[y, x + 1] + kbuf[y + 2, x + 1]
                + zsum(kbuf[1 + y, x + 1])
            )
        skap[x] = jnp.concatenate(parts, axis=1)

    def at_tile(it):
        return pl.ds(pl.multiple_of(it * TILE, TILE), TILE)

    def weighted(products, weights):
        total = products[:TILE] * weights[0:1]
        for k in range(1, modes):
            total = total + products[k * TILE:(k + 1) * TILE] * weights[k:k + 1]
        return total

    def mix(it, operand):
        return jnp.dot(m2[it, :, :operand.shape[0]], operand, preferred_element_type=f32)

    def interior(buf):
        @pl.loop(0, nx)
        def _(x):
            field, kap, sk = row(buf, x + 1), row(kbuf, x + 1), skap[x]

            @pl.loop(0, tiles)
            def _(it):
                products = mix(it, field)
                acc[x, at_tile(it)] = weighted(products, sk)
                w[x + 1, at_tile(it)] = weighted(products, kap)

    def borders(buf):
        for x in (0, nx + 1):
            field, kap = row(buf, x), row(kbuf, x)

            @pl.loop(0, tiles)
            def _(it, x=x, field=field, kap=kap):
                w[x, at_tile(it)] = weighted(mix(it, field), kap)

        @pl.loop(0, nx)
        def _(x):
            field = jnp.concatenate([buf[0, x + 1], buf[yl + 1, x + 1]], axis=1)
            kap = jnp.concatenate([kbuf[0, x + 1], kbuf[yl + 1, x + 1]], axis=1)

            @pl.loop(0, tiles)
            def _(it):
                wy[x, at_tile(it)] = weighted(mix(it, field), kap)

    def finish(buf, x, store):
        parts = []
        for y in range(yl):
            centre = buf[1 + y, x + 1].astype(f32)
            near = (
                buf[1 + y, x].astype(f32) + buf[1 + y, x + 2].astype(f32)
                + buf[y, x + 1].astype(f32) + buf[y + 2, x + 1].astype(f32)
            )
            parts.append(6.0 * centre - (near + zsum(centre)))
        lap = jnp.concatenate(parts, axis=1)
        high = lap.astype(bf16)
        low = (lap - high.astype(f32)).astype(bf16)
        both = jnp.concatenate([high, low], axis=0)
        kap = row(kbuf, x + 1)

        @pl.loop(0, tiles)
        def _(it):
            at = at_tile(it)
            total = acc[x, at] + weighted(mix(it, both), kap)
            total = total - (w[x, at] + w[x + 2, at])
            centre = w[x + 1, at]
            sides = wy[x, at]
            for y in range(yl):
                here = slice(y * nz, (y + 1) * nz)
                below = sides[:, :nz] if y == 0 else centre[:, (y - 1) * nz:y * nz]
                above = sides[:, nz:] if y == yl - 1 else centre[:, (y + 1) * nz:(y + 2) * nz]
                value = total[:, here] - (below + above + zsum(centre[:, here]))
                store(y, at, (0.5 * value).astype(bf16))

    def out_copy(which, src, out, d, src_dev, peer, srcx, dstx):
        return pltpu.make_async_remote_copy(
            src_ref=src(srcx, pl.ds(pl.multiple_of(d * cl, cl), cl)),
            dst_ref=out.at[pl.ds(src_dev * yl, yl), dstx],
            send_sem=out_send.at[which, d], recv_sem=out_recv.at[which, src_dev],
            device_id={"chaos": peer}, device_id_type=MESH,
        )

    def own_copy(which, src, out, srcx, dstx):
        return pltpu.make_async_copy(
            src(srcx, pl.ds(pl.multiple_of(me * cl, cl), cl)),
            out.at[pl.ds(me * yl, yl), dstx],
            local_sem.at[1 + which],
        )

    def out_start(which, src, out, srcx, dstx):
        @pl.loop(1, n)
        def _(s):
            d = lax.rem(me + s, n)
            out_copy(which, src, out, d, me, d, srcx, dstx).start()

        own_copy(which, src, out, srcx, dstx).start()

    def out_wait(which, src, out, srcx, dstx):
        @pl.loop(1, n)
        def _(s):
            d = lax.rem(me + s, n)
            copy = out_copy(which, src, out, d, d, d, srcx, dstx)
            copy.wait_send()
            copy.wait_recv()

        own_copy(which, src, out, srcx, dstx).wait()

    def first_at(xs, cs):
        return fbuf.at[rows, xs, cs]

    def second_at(xs, cs):
        return sbuf.at[:, xs, cs]

    @pl.loop(1, n)
    def _(s):
        d = lax.rem(me + s, n)
        in_copy(d, d, d).wait_recv()

    own_in.wait()
    for index in range(4):
        halo_start(vbuf, vhalo_send, vhalo_recv, index)
    interior(vbuf)
    halo_wait_recv(vbuf, vhalo_send, vhalo_recv)
    borders(vbuf)

    @pl.loop(0, nx)
    def _(x):
        def store(y, at, value):
            fbuf[1 + y, x + 1, at] = value

        finish(vbuf, x, store)
        for index in range(2):
            halo_start(fbuf, fhalo_send, fhalo_recv, index, x + 1)

        @pl.when(x == 0)
        def _():
            halo_start(fbuf, fhalo_send, fhalo_recv, 2)

        @pl.when(x == nx - 1)
        def _():
            halo_start(fbuf, fhalo_send, fhalo_recv, 3)

        out_start(0, first_at, out1, x + 1, x)

    interior(fbuf)
    halo_wait_recv(fbuf, fhalo_send, fhalo_recv)
    borders(fbuf)

    @pl.loop(0, nx)
    def _(x):
        def store(y, at, value):
            sbuf[y, x, at] = value

        finish(fbuf, x, store)
        out_start(1, second_at, out2, x, x)

    @pl.loop(1, n)
    def _(s):
        d = lax.rem(me + s, n)
        in_copy(d, d, d).wait_send()

    halo_wait_send(kbuf, khalo_send, khalo_recv)
    halo_wait_send(vbuf, vhalo_send, vhalo_recv)
    halo_wait_send(fbuf, fhalo_send, fhalo_recv)
    out_wait(0, first_at, out1, inner, pl.ds(0, nx))
    out_wait(1, second_at, out2, pl.ds(0, nx), pl.ds(0, nx))


def local(n, slabs, chaos_field, conductivity, triple_tensor, block_pattern):
    cl, nx, ny, nz = chaos_field.shape
    modes, coeffs, _ = triple_tensor.shape
    yl = ny // n
    kpad = -(-modes // 8) * 8
    block = coeffs // block_pattern.shape[0]
    f32, bf16 = jnp.float32, jnp.bfloat16
    mask = jnp.repeat(jnp.repeat(block_pattern, block, 0), block, 1).astype(bf16)
    vt = jnp.transpose(chaos_field, (2, 1, 0, 3))
    kt = jnp.pad(jnp.transpose(conductivity, (2, 1, 0, 3)), ((0, 0), (0, 0), (0, kpad - modes), (0, 0)))
    dma, vmem = pltpu.SemaphoreType.DMA, pltpu.VMEM
    out = jax.ShapeDtypeStruct((ny, nx, cl, nz), bf16)
    whole = pl.BlockSpec(memory_space=pltpu.VMEM)
    anywhere = pl.BlockSpec(memory_space=pl.ANY)
    first, second = pl.pallas_call(
        functools.partial(kernel, n, slabs, modes),
        out_shape=(out, out),
        in_specs=[anywhere, whole, whole, whole],
        out_specs=(anywhere, anywhere),
        scratch_shapes=[
            vmem((yl + 2, nx + 2, coeffs, nz), bf16),
            vmem((yl + 2, nx + 2, coeffs, nz), bf16),
            vmem((yl, nx, coeffs, nz), bf16),
            vmem((yl + 2, nx + 2, kpad, nz), f32),
            vmem((nx, kpad, yl * nz), f32),
            vmem((coeffs // TILE, modes * TILE, 2 * coeffs), bf16),
            vmem((nx, coeffs, yl * nz), f32),
            vmem((nx + 2, coeffs, yl * nz), f32),
            vmem((nx, coeffs, 2 * nz), f32),
            dma((n,)), dma((n,)),
            dma((4,)), dma((4,)), dma((4,)), dma((4,)), dma((4,)), dma((4,)),
            dma((2, n)), dma((2, n)), dma((3,)),
        ],
        compiler_params=pltpu.CompilerParams(
            collective_id=0, has_side_effects=True, vmem_limit_bytes=48 * 1024 * 1024,
        ),
    )(vt, triple_tensor, mask, kt)
    return jnp.transpose(first, (2, 1, 0, 3)), jnp.transpose(second, (2, 1, 0, 3))


def solution(mesh):
    n, slabs = mesh.shape["chaos"], mesh.shape["space"]
    return jax.shard_map(
        functools.partial(local, n, slabs),
        mesh=mesh,
        in_specs=(P("chaos", "space", None, None), P(None, "space", "chaos", None), P(), P()),
        out_specs=(P("chaos", "space", None, None), P("chaos", "space", None, None)),
        check_vma=False,
    )
```

time: 726 us -> 138 us (0.19)
  waiting for transfers between devices: 573 us -> 0 us
  Pallas kernels: 0 us -> 130 us
  matrix products: 58.1 us -> 0 us
  blocking collectives: 33.1 us -> 0 us
  local copies, waits for them, and re-layouts: 29.4 us -> 6.61 us
  between operations: 14.4 us -> 0.68 us
  starting transfers between devices: 11.8 us -> 0 us
    reduce_scatter x2 -> x0, waiting for transfers between devices: 570 us -> none  [product(): lax.psum_scatter(jnp.einsum('kij,kjxyz->ixyz', columns, applied, precisio...]
    pallas_call x0 -> x1, Pallas kernels: none -> 130 us  [local(): pl.pallas_call(functools.partial(kernel, n, slabs, modes), out_shape=(out...]
    dot_general x2 -> x0, matrix products: 58.1 us -> none  [product(): jnp.einsum('kij,kjxyz->ixyz', columns, applied, precision=lax.Precision.H...]
    all_gather x1 -> x0, blocking collectives: 33.1 us -> none  [local(): gathered = lax.all_gather(conductivity, 'chaos', axis=2, tiled=True)]
    slice x14 -> x0, local copies, waits for them, and re-layouts: 15.5 us -> none  [the longest x3 4.67 us: neighbours(): ypad[..., :-2, :]]
    ppermute x6 -> x0, starting transfers between devices: 11.7 us -> none  [the longest x3 7.87 us: padded_2(): before = lax.ppermute(last, axis, up)]
  transfers between devices with their start and end apart: 8 -> 0, of which waited for: 3 -> 0; matrix products, arithmetic and copies ran while one was open for 2% -> 0% of each run, Pallas kernels for 0% -> 0%
where the time goes in v1:
time: 138 us
  Pallas kernels  130 us (94%)
  local copies, waits for them, and re-layouts  6.61 us (5%)
    pallas_call x1, Pallas kernels, local(): pl.pallas_call(functools.partial(kernel, n, slabs, modes), out_shape=(out...  130 us
    unnamed x6, local copies, waits for them, and re-layouts  6.23 us

profile of v1, /device:TPU:0, one launch (start us, length us, event | category | flops | bytes accessed | tf_op | source)
XLA Modules:
  0.0 138.1 jit_solution(6894502109356095822)
XLA Ops:
  0.6 0.7 convert_element_type.9
  1.3 0.1 copy.11
  1.4 0.1 broadcast_in_dim.6
  1.5 0.1 convert_element_type.10
  1.6 0.0 copy-start
  1.6 0.1 copy.13.mask
  1.7 1.0 copy.19
  2.8 1.9 %copy.18 = bf16[32,8,16,128]{3,0,1,2:T(8,128)(2,1)S(1)} copy(bf16[32,8,16,128]{3,2,1,0:T(8,128)(2,1)} %param.4) | data formatting | bytes 2097152 | tf_op args[0]
  4.7 0.0 copy-done
  4.7 130.1 %shard_map.59 = (bf16[16,8,32,128]{3,2,1,0:T(8,128)(2,1)S(1)}, bf16[16,8,32,128]{3,2,1,0:T(8,128)(2,1)S(1)}) custom-call(bf16[16,8,32,128]{3,2,1,0:T(8,128)(2,1)S(1)} %bitcast.11, bf16[11,256,256]{2,1,0:T(8,128)(2,1)S(1)} %copy-done, bf16[256,256]{1,0:T(8,128)(2,1)S(1)} %copy.13.mask, f32[2,8,16,128]{3,2,1,0:T(8,128)S(1)} %pad.4.kt), custom_call_target="tpu_custom_call" | custom-call | tf_op jit(solution)/shard_map/pallas_call | solution.py:344
  134.8 1.6 %copy.14 = bf16[32,8,16,128]{3,2,1,0:T(8,128)(2,1)} copy(bf16[32,8,16,128]{3,0,1,2:T(8,128)(2,1)S(1)} %bitcast.13) | data formatting | bytes 2097152
  136.4 1.6 %copy.15 = bf16[32,8,16,128]{3,2,1,0:T(8,128)(2,1)} copy(bf16[32,8,16,128]{3,0,1,2:T(8,128)(2,1)S(1)} %bitcast.12) | data formatting | bytes 2097152
  (2 shorter events, 0.0 us)
Async XLA Ops:
  1.6 3.1 %copy-start = (bf16[11,256,256]{2,1,0:T(8,128)(2,1)S(1)}, bf16[11,256,256]{2,1,0:T(8,128)(2,1)}, u32[]{:S(2)}) copy-start(bf16[11,256,256]{2,1,0:T(8,128)(2,1)} %tensor.1) | copy-start | bytes 4325380

commit v2 on v1

v2 whole, which is shorter than its diff:
```python
import functools

import jax
import jax.numpy as jnp
from jax import lax
from jax.experimental import pallas as pl
from jax.experimental.pallas import tpu as pltpu
from jax.sharding import PartitionSpec as P

MESH = pl.DeviceIdType.MESH
TILE = 64
BANDS = 4


def kernel(
    n, slabs, modes, vt, tensor, mask, kt, out1, out2,
    vbuf, fbuf, sbuf, kbuf, skap, m2, acc, w, wy,
    in_send, in_recv, own_sem, kx_send, kx_recv, ky_send, ky_recv, vy_send, vy_recv, fy_send, fy_recv,
    kh_send, kh_recv, vh_send, vh_recv, fh_send, fh_recv, out_send, out_recv, local_sem,
):
    me = lax.axis_index("chaos")
    sp = lax.axis_index("space")
    yl, nx = vbuf.shape[0] - 2, vbuf.shape[1] - 2
    coeffs, nz = vbuf.shape[2], vbuf.shape[3]
    cl = coeffs // n
    group = n // BANDS
    krows = kt.shape[0]
    tiles = coeffs // TILE
    f32, bf16 = jnp.float32, jnp.bfloat16
    band, part = me // group, me % group
    gx = sp * group + part
    down, up = band > 0, band < BANDS - 1
    left, right = gx > 0, gx < slabs * group - 1
    lx, rx = jnp.maximum(gx - 1, 0), gx + 1
    left_peer = {"space": lx // group, "chaos": band * group + lx % group}
    right_peer = {"space": rx // group, "chaos": band * group + rx % group}
    inner, rows = pl.ds(1, nx), pl.ds(1, yl)
    other = lax.rem(me + 1, n)

    for buf in (vbuf, fbuf, kbuf):
        @pl.when(jnp.logical_not(down))
        def _(buf=buf):
            buf[0] = jnp.zeros(buf.shape[1:], buf.dtype)

        @pl.when(jnp.logical_not(up))
        def _(buf=buf):
            buf[yl + 1] = jnp.zeros(buf.shape[1:], buf.dtype)

        @pl.when(jnp.logical_not(left))
        def _(buf=buf):
            for y in range(yl):
                buf[1 + y, 0] = jnp.zeros(buf.shape[2:], buf.dtype)

        @pl.when(jnp.logical_not(right))
        def _(buf=buf):
            for y in range(yl):
                buf[1 + y, nx + 1] = jnp.zeros(buf.shape[2:], buf.dtype)

    far_left = jnp.logical_and(left, part == 0)
    far_right = jnp.logical_and(right, part == group - 1)
    barrier = pltpu.get_barrier_semaphore()

    @pl.loop(1, n)
    def _(s):
        pl.semaphore_signal(barrier, inc=1, device_id={"chaos": lax.rem(me + s, n)}, device_id_type=MESH)

    for cond, peer in ((far_left, left_peer), (far_right, right_peer)):
        @pl.when(cond)
        def _(peer=peer):
            pl.semaphore_signal(barrier, inc=1, device_id=peer, device_id_type=MESH)

    pl.semaphore_wait(barrier, n - 1 + far_left.astype(jnp.int32) + far_right.astype(jnp.int32))

    def k_copy(p, src_part, peer):
        return pltpu.make_async_remote_copy(
            src_ref=kt.at[:, pl.ds(p * nx, nx)],
            dst_ref=kbuf.at[pl.ds(1 + src_part * krows, krows), inner],
            send_sem=kx_send.at[p], recv_sem=kx_recv.at[src_part],
            device_id={"chaos": peer}, device_id_type=MESH,
        )

    own_k = pltpu.make_async_copy(
        kt.at[:, pl.ds(part * nx, nx)], kbuf.at[pl.ds(1 + part * krows, krows), inner], local_sem.at[0],
    )
    own_k.start()

    @pl.loop(1, group)
    def _(s):
        p = lax.rem(part + s, group)
        k_copy(p, part, band * group + p).start()

    def my_rows(device):
        return pl.ds(pl.multiple_of(device * cl, cl), cl)

    def in_copy(d, src_dev, x):
        return pltpu.make_async_remote_copy(
            src_ref=vt.at[pl.ds((d // group) * yl, yl), (d % group) * nx + x],
            dst_ref=vbuf.at[rows, 1 + x, my_rows(src_dev)],
            send_sem=in_send.at[x, d], recv_sem=in_recv.at[x, src_dev],
            device_id={"chaos": d}, device_id_type=MESH,
        )

    def own_in(x):
        return pltpu.make_async_copy(
            vt.at[pl.ds(band * yl, yl), part * nx + x], vbuf.at[rows, 1 + x, my_rows(me)], own_sem.at[x],
        )

    @pl.loop(0, nx)
    def _(x):
        @pl.loop(1, n)
        def _(s):
            in_copy(lax.rem(me + s, n), me, x).start()

        own_in(x).start()

    def y_halo(buf, send, recv, index, target, xs, slot):
        src, dst = ((1, yl + 1), (yl, 0))[index]
        return pltpu.make_async_remote_copy(
            src_ref=buf.at[src, xs], dst_ref=buf.at[dst, xs],
            send_sem=send.at[index, slot], recv_sem=recv.at[index, slot],
            device_id=target, device_id_type=MESH,
        )

    def x_halo(buf, send, recv, index, target):
        src, dst = ((1, nx + 1), (nx, 0))[index]
        return pltpu.make_async_remote_copy(
            src_ref=buf.at[rows, src], dst_ref=buf.at[rows, dst],
            send_sem=send.at[index], recv_sem=recv.at[index],
            device_id=target, device_id_type=MESH,
        )

    y_sends = ((down, {"chaos": me - group}), (up, {"chaos": me + group}))
    x_sends = ((left, left_peer), (right, right_peer))
    y_arrives, x_arrives = (up, down), (right, left)

    def y_start(buf, send, recv, xs, slot):
        for index, (cond, target) in enumerate(y_sends):
            @pl.when(cond)
            def _(index=index, target=target):
                y_halo(buf, send, recv, index, target, xs, slot).start()

    def y_wait(buf, send, recv, xs, slot):
        for index, cond in enumerate(y_arrives):
            @pl.when(cond)
            def _(index=index):
                y_halo(buf, send, recv, index, {"chaos": other}, xs, slot).wait_recv()

    def y_sent(buf, send, recv, xs, slot):
        for index, (cond, _) in enumerate(y_sends):
            @pl.when(cond)
            def _(index=index):
                y_halo(buf, send, recv, index, {"chaos": other}, xs, slot).wait_send()

    def x_start(buf, send, recv, index, also=True):
        cond, target = x_sends[index]

        @pl.when(jnp.logical_and(cond, also))
        def _():
            x_halo(buf, send, recv, index, target).start()

    def x_wait(buf, send, recv, index):
        @pl.when(x_arrives[index])
        def _():
            x_halo(buf, send, recv, index, {"chaos": other}).wait_recv()

    def x_sent(buf, send, recv):
        for index in range(2):
            @pl.when(x_sends[index][0])
            def _(index=index):
                x_halo(buf, send, recv, index, {"chaos": other}).wait_send()

    own_k.wait()

    @pl.loop(1, group)
    def _(s):
        p = lax.rem(part + s, group)
        k_copy(p, p, band * group + p).wait_recv()

    y_start(kbuf, ky_send, ky_recv, inner, 0)
    for index in range(2):
        x_start(kbuf, kh_send, kh_recv, index)

    @pl.loop(0, tiles)
    def _(it):
        at = pl.ds(pl.multiple_of(it * TILE, TILE), TILE)
        kept = mask[at]
        for k in range(modes):
            value = tensor[k, at] * kept
            m2[it, k * TILE:(k + 1) * TILE, :coeffs] = value
            m2[it, k * TILE:(k + 1) * TILE, coeffs:] = value

    lane = lax.broadcasted_iota(jnp.int32, (1, nz), 1)

    def zsum(block):
        before = jnp.where(lane == 0, 0.0, pltpu.roll(block, 1, 1))
        after = jnp.where(lane == nz - 1, 0.0, pltpu.roll(block, nz - 1, 1))
        return before + after

    def row(buf, x, first=1):
        return jnp.concatenate([buf[first + y, x] for y in range(yl)], axis=1)

    y_wait(kbuf, ky_send, ky_recv, inner, 0)
    for index in range(2):
        x_wait(kbuf, kh_send, kh_recv, index)

    @pl.loop(0, nx)
    def _(x):
        parts = []
        for y in range(yl):
            parts.append(
                kbuf[1 + y, x] + kbuf[1 + y, x + 2] + kbuf[y, x + 1] + kbuf[y + 2, x + 1]
                + zsum(kbuf[1 + y, x + 1])
            )
        skap[x] = jnp.concatenate(parts, axis=1)

    def at_tile(it):
        return pl.ds(pl.multiple_of(it * TILE, TILE), TILE)

    def weighted(products, weights):
        total = products[:TILE] * weights[0:1]
        for k in range(1, modes):
            total = total + products[k * TILE:(k + 1) * TILE] * weights[k:k + 1]
        return total

    def mix(it, operand):
        return jnp.dot(m2[it, :, :operand.shape[0]], operand, preferred_element_type=f32)

    def interior(buf, x):
        field, kap, sk = row(buf, x + 1), row(kbuf, x + 1), skap[x]

        @pl.loop(0, tiles, unroll=True)
        def _(it):
            products = mix(it, field)
            acc[x, at_tile(it)] = weighted(products, sk)
            w[x + 1, at_tile(it)] = weighted(products, kap)

    def x_border(buf, x):
        field, kap = row(buf, x), row(kbuf, x)

        @pl.loop(0, tiles, unroll=True)
        def _(it):
            w[x, at_tile(it)] = weighted(mix(it, field), kap)

    def y_border(buf, x):
        field = jnp.concatenate([buf[0, x + 1], buf[yl + 1, x + 1]], axis=1)
        kap = jnp.concatenate([kbuf[0, x + 1], kbuf[yl + 1, x + 1]], axis=1)

        @pl.loop(0, tiles, unroll=True)
        def _(it):
            wy[x, at_tile(it)] = weighted(mix(it, field), kap)

    def finish(buf, x, store):
        parts = []
        for y in range(yl):
            centre = buf[1 + y, x + 1].astype(f32)
            near = (
                buf[1 + y, x].astype(f32) + buf[1 + y, x + 2].astype(f32)
                + buf[y, x + 1].astype(f32) + buf[y + 2, x + 1].astype(f32)
            )
            parts.append(6.0 * centre - (near + zsum(centre)))
        lap = jnp.concatenate(parts, axis=1)
        high = lap.astype(bf16)
        low = (lap - high.astype(f32)).astype(bf16)
        both = jnp.concatenate([high, low], axis=0)
        kap = row(kbuf, x + 1)

        @pl.loop(0, tiles, unroll=True)
        def _(it):
            at = at_tile(it)
            total = acc[x, at] + weighted(mix(it, both), kap)
            total = total - (w[x, at] + w[x + 2, at])
            centre = w[x + 1, at]
            sides = wy[x, at]
            for y in range(yl):
                here = slice(y * nz, (y + 1) * nz)
                below = sides[:, :nz] if y == 0 else centre[:, (y - 1) * nz:y * nz]
                above = sides[:, nz:] if y == yl - 1 else centre[:, (y + 1) * nz:(y + 2) * nz]
                value = total[:, here] - (below + above + zsum(centre[:, here]))
                store(y, at, (0.5 * value).astype(bf16))

    def out_copy(which, src, out, d, src_dev, srcx, dstx, width):
        return pltpu.make_async_remote_copy(
            src_ref=src(srcx, my_rows(d)),
            dst_ref=out.at[pl.ds((src_dev // group) * yl, yl), pl.ds((src_dev % group) * nx + dstx, width)],
            send_sem=out_send.at[which, d], recv_sem=out_recv.at[which, src_dev],
            device_id={"chaos": d}, device_id_type=MESH,
        )

    def own_copy(which, src, out, srcx, dstx, width):
        return pltpu.make_async_copy(
            src(srcx, my_rows(me)),
            out.at[pl.ds(band * yl, yl), pl.ds(part * nx + dstx, width)],
            local_sem.at[1 + which],
        )

    def out_start(which, src, out, srcx, dstx):
        @pl.loop(1, n)
        def _(s):
            out_copy(which, src, out, lax.rem(me + s, n), me, pl.ds(srcx, 1), dstx, 1).start()

        own_copy(which, src, out, pl.ds(srcx, 1), dstx, 1).start()

    def out_wait(which, src, out, srcx):
        @pl.loop(1, n)
        def _(s):
            d = lax.rem(me + s, n)
            copy = out_copy(which, src, out, d, d, srcx, 0, nx)
            copy.wait_send()
            copy.wait_recv()

        own_copy(which, src, out, srcx, 0, nx).wait()

    def first_at(xs, cs):
        return fbuf.at[rows, xs, cs]

    def second_at(xs, cs):
        return sbuf.at[:, xs, cs]

    @pl.loop(0, nx)
    def _(x):
        @pl.loop(1, n)
        def _(s):
            d = lax.rem(me + s, n)
            in_copy(d, d, x).wait_recv()

        own_in(x).wait()
        y_start(vbuf, vy_send, vy_recv, x + 1, x)
        x_start(vbuf, vh_send, vh_recv, 0, x == 0)
        x_start(vbuf, vh_send, vh_recv, 1, x == nx - 1)
        interior(vbuf, x)

    x_wait(vbuf, vh_send, vh_recv, 1)
    x_border(vbuf, 0)
    x_wait(vbuf, vh_send, vh_recv, 0)
    x_border(vbuf, nx + 1)

    @pl.loop(0, nx)
    def _(x):
        def store(y, at, value):
            fbuf[1 + y, x + 1, at] = value

        y_wait(vbuf, vy_send, vy_recv, x + 1, x)
        y_border(vbuf, x)
        finish(vbuf, x, store)
        y_start(fbuf, fy_send, fy_recv, x + 1, x)
        x_start(fbuf, fh_send, fh_recv, 0, x == 0)
        x_start(fbuf, fh_send, fh_recv, 1, x == nx - 1)
        out_start(0, first_at, out1, x + 1, x)

    interior(fbuf, 0)
    x_wait(fbuf, fh_send, fh_recv, 1)
    x_border(fbuf, 0)

    @pl.loop(0, nx)
    def _(x):
        def store(y, at, value):
            sbuf[y, x, at] = value

        @pl.when(x < nx - 1)
        def _():
            interior(fbuf, x + 1)

        @pl.when(x == nx - 1)
        def _():
            x_wait(fbuf, fh_send, fh_recv, 0)
            x_border(fbuf, nx + 1)

        y_wait(fbuf, fy_send, fy_recv, x + 1, x)
        y_border(fbuf, x)
        finish(fbuf, x, store)
        out_start(1, second_at, out2, x, x)

    @pl.loop(0, nx)
    def _(x):
        @pl.loop(1, n)
        def _(s):
            in_copy(lax.rem(me + s, n), me, x).wait_send()

        y_sent(vbuf, vy_send, vy_recv, x + 1, x)
        y_sent(fbuf, fy_send, fy_recv, x + 1, x)

    @pl.loop(1, group)
    def _(s):
        p = lax.rem(part + s, group)
        k_copy(p, part, band * group + p).wait_send()

    y_sent(kbuf, ky_send, ky_recv, inner, 0)
    x_sent(kbuf, kh_send, kh_recv)
    x_sent(vbuf, vh_send, vh_recv)
    x_sent(fbuf, fh_send, fh_recv)
    out_wait(0, first_at, out1, inner)
    out_wait(1, second_at, out2, pl.ds(0, nx))


def local(n, slabs, chaos_field, conductivity, triple_tensor, block_pattern):
    cl, slab, ny, nz = chaos_field.shape
    modes, coeffs, _ = triple_tensor.shape
    yl, nx, group = ny // BANDS, slab * BANDS // n, n // BANDS
    kpad = -(-modes // 8) * 8
    block = coeffs // block_pattern.shape[0]
    f32, bf16 = jnp.float32, jnp.bfloat16
    mask = jnp.repeat(jnp.repeat(block_pattern, block, 0), block, 1).astype(bf16)
    vt = jnp.transpose(chaos_field, (2, 1, 0, 3))
    kt = jnp.pad(jnp.transpose(conductivity, (2, 1, 0, 3)), ((0, 0), (0, 0), (0, kpad - modes), (0, 0)))
    dma, vmem = pltpu.SemaphoreType.DMA, pltpu.VMEM
    out = jax.ShapeDtypeStruct((ny, slab, cl, nz), bf16)
    whole = pl.BlockSpec(memory_space=pltpu.VMEM)
    anywhere = pl.BlockSpec(memory_space=pl.ANY)
    first, second = pl.pallas_call(
        functools.partial(kernel, n, slabs, modes),
        out_shape=(out, out),
        in_specs=[anywhere, whole, whole, anywhere],
        out_specs=(anywhere, anywhere),
        scratch_shapes=[
            vmem((yl + 2, nx + 2, coeffs, nz), bf16),
            vmem((yl + 2, nx + 2, coeffs, nz), bf16),
            vmem((yl, nx, coeffs, nz), bf16),
            vmem((yl + 2, nx + 2, kpad, nz), f32),
            vmem((nx, kpad, yl * nz), f32),
            vmem((coeffs // TILE, modes * TILE, 2 * coeffs), bf16),
            vmem((nx, coeffs, yl * nz), f32),
            vmem((nx + 2, coeffs, yl * nz), f32),
            vmem((nx, coeffs, 2 * nz), f32),
            dma((nx, n)), dma((nx, n)), dma((nx,)), dma((group,)), dma((group,)),
            dma((2, 1)), dma((2, 1)), dma((2, nx)), dma((2, nx)), dma((2, nx)), dma((2, nx)),
            dma((2,)), dma((2,)), dma((2,)), dma((2,)), dma((2,)), dma((2,)),
            dma((2, n)), dma((2, n)), dma((3,)),
        ],
        compiler_params=pltpu.CompilerParams(
            collective_id=0, has_side_effects=True, vmem_limit_bytes=48 * 1024 * 1024,
        ),
    )(vt, triple_tensor, mask, kt)
    return jnp.transpose(first, (2, 1, 0, 3)), jnp.transpose(second, (2, 1, 0, 3))


def solution(mesh):
    n, slabs = mesh.shape["chaos"], mesh.shape["space"]
    return jax.shard_map(
        functools.partial(local, n, slabs),
        mesh=mesh,
        in_specs=(P("chaos", "space", None, None), P(None, "space", "chaos", None), P(), P()),
        out_specs=(P("chaos", "space", None, None), P("chaos", "space", None, None)),
        check_vma=False,
    )
```

time: 138 us -> 105 us (0.76)
  Pallas kernels: 130 us -> 96.4 us
    pallas_call x1, Pallas kernels: 130 us -> 96.4 us  [local(): pl.pallas_call(functools.partial(kernel, n, slabs, modes), out_shape=(out...]
where the time goes in v2:
time: 105 us; the launch traced here: 104 us
  Pallas kernels  96.4 us (92%)
  local copies, waits for them, and re-layouts  6.61 us (6%)
    pallas_call x1, Pallas kernels, local(): pl.pallas_call(functools.partial(kernel, n, slabs, modes), out_shape=(out...  96.4 us
    unnamed x6, local copies, waits for them, and re-layouts  6.23 us

profile of v2, /device:TPU:0, one launch (start us, length us, event | category | flops | bytes accessed | tf_op | source)
XLA Modules:
  0.0 104.4 jit_solution(10664698886082626846)
XLA Ops:
  0.6 0.7 convert_element_type.9
  1.3 0.1 copy.11
  1.4 0.1 broadcast_in_dim.6
  1.5 0.1 convert_element_type.10
  1.6 0.0 copy-start
  1.6 0.1 copy.13.mask
  1.7 1.0 copy.19
  2.8 1.9 %copy.18 = bf16[32,8,16,128]{3,0,1,2:T(8,128)(2,1)S(1)} copy(bf16[32,8,16,128]{3,2,1,0:T(8,128)(2,1)} %param.4) | data formatting | bytes 2097152 | tf_op args[0]
  4.7 0.0 copy-done
  4.7 96.4 %shard_map.59 = (bf16[16,8,32,128]{3,2,1,0:T(8,128)(2,1)S(1)}, bf16[16,8,32,128]{3,2,1,0:T(8,128)(2,1)S(1)}) custom-call(bf16[16,8,32,128]{3,2,1,0:T(8,128)(2,1)S(1)} %bitcast.11, bf16[11,256,256]{2,1,0:T(8,128)(2,1)S(1)} %copy-done, bf16[256,256]{1,0:T(8,128)(2,1)S(1)} %copy.13.mask, f32[2,8,16,128]{3,2,1,0:T(8,128)S(1)} %pad.4.kt), custom_call_target="tpu_custom_call" | custom-call | tf_op jit(solution)/shard_map/pallas_call | solution.py:409
  101.1 1.6 %copy.14 = bf16[32,8,16,128]{3,2,1,0:T(8,128)(2,1)} copy(bf16[32,8,16,128]{3,0,1,2:T(8,128)(2,1)S(1)} %bitcast.13) | data formatting | bytes 2097152
  102.7 1.6 %copy.15 = bf16[32,8,16,128]{3,2,1,0:T(8,128)(2,1)} copy(bf16[32,8,16,128]{3,0,1,2:T(8,128)(2,1)S(1)} %bitcast.12) | data formatting | bytes 2097152
  (2 shorter events, 0.0 us)
Async XLA Ops:
  1.6 3.1 %copy-start = (bf16[11,256,256]{2,1,0:T(8,128)(2,1)S(1)}, bf16[11,256,256]{2,1,0:T(8,128)(2,1)}, u32[]{:S(2)}) copy-start(bf16[11,256,256]{2,1,0:T(8,128)(2,1)} %tensor.1) | copy-start | bytes 4325380
